TPU v7x, 256 devices: a whole 4x4x8 slice. The times are simulated.
256 devices in a mesh: mid: 16 (over y, z_lo, core), leaf: 16 (over x, z_hi).
Axes of the slice: x: 4, y: 4, z: 8 (z_hi: 4, z_lo: 2; z = z_hi * 2 + z_lo), core: 2. Of those that a mesh axis runs over, the one named last changes fastest.
Arguments:
- queries: bfloat16 [65536, 4096], P(('mid', 'leaf')), may hold values from -128 to 128
- out_grad: bfloat16 [65536, 4096], P(('mid', 'leaf')), may hold values from -6 to 6
- leaf_keys: bfloat16 [65536, 1024], P(('mid', 'leaf')), may hold values from -6 to 6
- leaf_values: bfloat16 [65536, 1024], P(('mid', 'leaf')), may hold values from -6 to 6
- mid_keys: bfloat16 [4096, 1024], P(('mid', 'leaf')), may hold values from -6 to 6
- mid_values: bfloat16 [4096, 1024], P(('mid', 'leaf')), may hold values from -6 to 6
- root_keys: bfloat16 [512, 1024], P(('mid', 'leaf')), may hold values from -4 to 4
- root_values: bfloat16 [512, 1024], P(('mid', 'leaf')), may hold values from -6 to 6
- mid_len: int32 [16], P('mid'), may hold values from 1 to 256, 3072 in all
- leaf_len: int32 [256], P(('mid', 'leaf')), may hold values from 1 to 256, 40960 in all
Outputs:
- query_grad: bfloat16 [65536, 4096], P(('mid', 'leaf'))
- leaf_key_grad: bfloat16 [65536, 1024], P(('mid', 'leaf'))
- leaf_value_grad: bfloat16 [65536, 1024], P(('mid', 'leaf'))
- mid_key_grad: float32 [4096, 1024], P(('mid', 'leaf'))
- mid_value_grad: float32 [4096, 1024], P(('mid', 'leaf'))
- root_key_grad: float32 [512, 1024], P(('mid', 'leaf'))
- root_value_grad: float32 [512, 1024], P(('mid', 'leaf'))
Inputs may be any that keep to these rules, and one draw needn't show every extreme that they name: `mid_len`: at least one mid branch has all 256 tokens live. `leaf_len`: at least one leaf has all 256 tokens live.
All inputs are finite; a program needn't handle non-finite values. No bound on the sum of `mid_len` or of `leaf_len` on one device may be relied on, other than what follows from the above.
Results may differ from a plain program's by a relative error of at most 0.013.
Values may be sent and summed in bfloat16 or wider, within the bound.
A program may use at most 128 MiB of HBM per device.

v0:
```python
import jax
import jax.numpy as jnp
from jax import lax
from jax.sharding import PartitionSpec as P

QH = 32
KVH = 8
HD = 128


def leaf_backward(
    queries, out_grad, all_keys, all_values, root_rows, mid_rows, mid_live, leaf_live
):
    leaf_rows = queries.shape[0]
    key_rows = all_keys.shape[0]
    heads_per = QH // KVH
    span_cols = heads_per * HD
    column = jnp.arange(key_rows, dtype=jnp.int32)[None, :]
    row_ids = jnp.arange(leaf_rows, dtype=jnp.int32)[:, None]
    offset = root_rows + mid_rows
    leaf_pos = column - offset
    in_root = column < root_rows
    in_mid = (column >= root_rows) & (column < offset) & (column - root_rows < mid_live)
    in_leaf = (leaf_pos >= 0) & (leaf_pos <= row_ids) & (leaf_pos < leaf_live)
    allowed = in_root | in_mid | in_leaf
    live_rows = (jnp.arange(leaf_rows, dtype=jnp.int32) < leaf_live).astype(jnp.float32)[
        None, :, None
    ]
    factor = HD ** (-0.5)

    def one_head(head_index, buffers):
        query_acc, key_acc, value_acc = buffers
        query_part = lax.dynamic_slice_in_dim(
            queries, head_index * span_cols, span_cols, 1
        ).reshape(leaf_rows, heads_per, HD)
        grad_part = lax.dynamic_slice_in_dim(
            out_grad, head_index * span_cols, span_cols, 1
        ).reshape(leaf_rows, heads_per, HD)
        key_part = lax.dynamic_slice_in_dim(all_keys, head_index * HD, HD, 1)
        value_part = lax.dynamic_slice_in_dim(all_values, head_index * HD, HD, 1)
        scores = factor * jnp.einsum(
            "igd,jd->gij", query_part, key_part, preferred_element_type=jnp.float32
        )
        scores = jnp.where(allowed[None], scores, -1e30)
        row_max = jnp.max(scores, axis=-1, keepdims=True)
        weights = jnp.exp(scores - row_max)
        probs = weights / jnp.sum(weights, axis=-1, keepdims=True) * live_rows
        probs_low = probs.astype(jnp.bfloat16)
        value_term = jnp.einsum(
            "gij,igd->jd", probs_low, grad_part, preferred_element_type=jnp.float32
        )
        dprobs = jnp.einsum(
            "igd,jd->gij", grad_part, value_part, preferred_element_type=jnp.float32
        )
        row_dots = jnp.sum(probs * dprobs, axis=-1, keepdims=True)
        dscores = (probs * (dprobs - row_dots)).astype(jnp.bfloat16)
        query_term = factor * jnp.einsum(
            "gij,jd->igd", dscores, key_part, preferred_element_type=jnp.float32
        )
        key_term = factor * jnp.einsum(
            "gij,igd->jd", dscores, query_part, preferred_element_type=jnp.float32
        )
        query_acc = lax.dynamic_update_slice_in_dim(
            query_acc,
            query_term.reshape(leaf_rows, span_cols).astype(jnp.bfloat16),
            head_index * span_cols,
            1,
        )
        key_acc = lax.dynamic_update_slice_in_dim(key_acc, key_term, head_index * HD, 1)
        value_acc = lax.dynamic_update_slice_in_dim(value_acc, value_term, head_index * HD, 1)
        return (query_acc, key_acc, value_acc)

    start = (
        jnp.zeros((leaf_rows, QH * HD), jnp.bfloat16),
        jnp.zeros((key_rows, KVH * HD), jnp.float32),
        jnp.zeros((key_rows, KVH * HD), jnp.float32),
    )
    return lax.fori_loop(0, KVH, one_head, start)


def on_device(
    queries,
    out_grad,
    leaf_keys,
    leaf_values,
    mid_keys,
    mid_values,
    root_keys,
    root_values,
    mid_len,
    leaf_len,
):
    root_k, root_v = (
        lax.all_gather(root_keys, ("mid", "leaf"), axis=0, tiled=True),
        lax.all_gather(root_values, ("mid", "leaf"), axis=0, tiled=True),
    )
    branch_k, branch_v = (
        lax.all_gather(mid_keys, "leaf", axis=0, tiled=True),
        lax.all_gather(mid_values, "leaf", axis=0, tiled=True),
    )
    root_rows = root_k.shape[0]
    mid_rows = branch_k.shape[0]
    all_keys = jnp.concatenate([root_k, branch_k, leaf_keys], 0)
    all_values = jnp.concatenate([root_v, branch_v, leaf_values], 0)
    query_grad, key_terms, value_terms = leaf_backward(
        queries, out_grad, all_keys, all_values, root_rows, mid_rows, mid_len[0], leaf_len[0]
    )
    offset = root_rows + mid_rows
    leaf_key_grad = key_terms[offset:].astype(jnp.bfloat16)
    leaf_value_grad = value_terms[offset:].astype(jnp.bfloat16)
    root_key_terms = key_terms[:root_rows]
    root_value_terms = value_terms[:root_rows]
    mid_key_terms = key_terms[root_rows:offset]
    mid_value_terms = value_terms[root_rows:offset]
    root_key_grad, root_value_grad = (
        lax.psum_scatter(root_key_terms, ("mid", "leaf"), scatter_dimension=0, tiled=True),
        lax.psum_scatter(root_value_terms, ("mid", "leaf"), scatter_dimension=0, tiled=True),
    )
    mid_key_grad, mid_value_grad = (
        lax.psum_scatter(mid_key_terms, "leaf", scatter_dimension=0, tiled=True),
        lax.psum_scatter(mid_value_terms, "leaf", scatter_dimension=0, tiled=True),
    )
    return (
        query_grad,
        leaf_key_grad,
        leaf_value_grad,
        mid_key_grad,
        mid_value_grad,
        root_key_grad,
        root_value_grad,
    )


def solution(mesh):
    in_specs = (
        P(("mid", "leaf"), None),
        P(("mid", "leaf"), None),
        P(("mid", "leaf"), None),
        P(("mid", "leaf"), None),
        P(("mid", "leaf"), None),
        P(("mid", "leaf"), None),
        P(("mid", "leaf"), None),
        P(("mid", "leaf"), None),
        P("mid"),
        P(("mid", "leaf")),
    )
    out_specs = (
        P(("mid", "leaf"), None),
        P(("mid", "leaf"), None),
        P(("mid", "leaf"), None),
        P(("mid", "leaf"), None),
        P(("mid", "leaf"), None),
        P(("mid", "leaf"), None),
        P(("mid", "leaf"), None),
    )
    return jax.shard_map(
        on_device, mesh=mesh, in_specs=in_specs, out_specs=out_specs, check_vma=False
    )
```

profile of v0, /device:TPU:8, one launch (start us, length us, event | category | flops | bytes accessed | tf_op | source)
XLA Modules:
  0.0 1676.8 jit_solution(2262667094924858593)
XLA Ops:
  10.0 49.7 %all_gather.13 = bf16[256,1024]{1,0:T(8,128)(2,1)S(1)} all-gather(bf16[16,1024]{1,0:T(8,128)(2,1)} %param.16), channel_id=1, replica_groups=mesh['mid'=16,'leaf'=16] {'leaf'}, dimensions={0}, use_global_device_ids=true | all-gather | bytes 557056 | tf_op jit(solution)/shard_map/all_gather | solution.py:98
  59.7 41.5 %all_gather.15 = bf16[256,1024]{1,0:T(8,128)(2,1)S(1)} all-gather(bf16[16,1024]{1,0:T(8,128)(2,1)} %param.17), channel_id=1, replica_groups=mesh['mid'=16,'leaf'=16] {'leaf'}, dimensions={0}, use_global_device_ids=true | all-gather | bytes 557056 | tf_op jit(solution)/shard_map/all_gather | solution.py:99
  101.2 435.3 %all-gather.5.cloned.1.call-done = bf16[256,2,1024]{2,1,0:T(2,128)(2,1)} async-done(((bf16[1,2,1024]{2,1,0:T(2,128)(2,1)}), bf16[256,2,1024]{2,1,0:T(2,128)(2,1)}) %all-gather.5.cloned.1.call-update) | async-done | bytes 1048592 | tf_op jit(solution)/shard_map/all_gather | solution.py:94
  538.0 2.5 pad_maximum_fusion
  540.6 523.7 %all-gather.7.cloned.1.call-done = bf16[256,2,1024]{2,1,0:T(2,128)(2,1)} async-done(((bf16[1,2,1024]{2,1,0:T(2,128)(2,1)}), bf16[256,2,1024]{2,1,0:T(2,128)(2,1)}) %all-gather.7.cloned.1.call-update) | async-done | bytes 1048592 | tf_op jit(solution)/shard_map/all_gather | solution.py:95
  1067.2 1.6 broadcast_in_dim.42.clone
  1068.8 2.5 broadcast.97.clone
  1071.3 2.5 broadcast.97
  1073.8 142.3 %while.18 = (s32[]{:T(128)}, bf16[256,4096]{1,0:T(8,128)(2,1)}, f32[1024,1024]{1,0:T(8,128)}, f32[1024,1024]{1,0:T(8,128)}, bf16[1024,1024]{1,0:T(8,128)(2,1)}, ...) while((s32[]{:T(128)}, bf16[256,4096]{1,0:T(8,128)(2,1)}, ...), condition=%wide.region_4.5_spmd.clone, body=%wide.region_0.4_spmd.clone.sunk | while | flops 1360396800 | bytes 55086412 | solution.py:78
  1076.9 4.4 fusion.95
  1081.3 3.9 fusion.100
  1085.2 1.7 fusion.96
  1090.0 1.6 fusion.99
  1094.7 4.4 fusion.95
  1099.1 3.9 fusion.100
  1103.0 1.7 fusion.96
  1107.8 1.6 fusion.99
  1112.5 4.4 fusion.95
  1116.9 3.9 fusion.100
  1120.8 1.7 fusion.96
  1130.2 4.4 fusion.95
  1134.7 3.9 fusion.100
  1138.6 1.7 fusion.96
  1143.4 1.5 fusion.99
  1148.0 4.4 fusion.95
  1152.4 3.9 fusion.100
  1156.3 1.7 fusion.96
  1161.2 1.5 fusion.99
  1165.8 4.4 fusion.95
  1170.2 3.9 fusion.100
  1174.1 1.7 fusion.96
  1178.9 1.5 fusion.99
  1183.6 4.4 fusion.95
  1188.0 3.9 fusion.100
  1191.9 1.7 fusion.96
  1196.7 1.5 fusion.99
  1201.4 4.4 fusion.95
  1205.8 3.9 fusion.100
  1209.7 1.7 fusion.96
  1214.5 1.5 fusion.99
  1216.0 3.3 slice.25
  1220.9 2.4 slice.23
  1223.3 2.3 slice.22
  1225.7 2.1 slice.30
  1227.8 2.1 slice.31
  1229.9 263.1 %all-reduce.5.cloned.1.call-done = (f32[512,1024]{1,0:T(8,128)}, f32[512,1024]{1,0:T(8,128)}) async-done(((f32[512,1024]{1,0:T(8,128)}, f32[512,1024]{1,0:T(8,128)}), (f32[512,1024]{1,0:T(8,128)}, f32[512,1024]{1,0:T(8,128)})) %all-reduce.5.cloned.1.call-update) | async-done | bytes 4194320
  1495.7 86.7 %reduce-scatter.5.cloned.1.call-done = f32[16,1024]{1,0:T(8,128)} async-done(((f32[256,1024]{1,0:T(8,128)}), f32[16,1024]{1,0:T(8,128)}) %reduce-scatter.5.cloned.1.call-update) | async-done | bytes 65552 | tf_op jit(solution)/shard_map/reduce_scatter | solution.py:121
  1582.3 87.9 %reduce-scatter.3.cloned.1.call-done = f32[16,1024]{1,0:T(8,128)} async-done(((f32[256,1024]{1,0:T(8,128)}), f32[16,1024]{1,0:T(8,128)}) %reduce-scatter.3.cloned.1.call-update) | async-done | bytes 65552 | tf_op jit(solution)/shard_map/reduce_scatter | solution.py:120
  (112 shorter events, 61.0 us)
Async XLA Ops:
  7.2 529.4 %all-gather.5.cloned.1.call-start = ((), (), s32[]{:S(2)}) async-start(), calls=%async_computation.4 | async-start | bytes 1052672 | tf_op jit(solution)/shard_map/all_gather | solution.py:94
  7.9 1056.4 %all-gather.7.cloned.1.call-start = ((), (), s32[]{:S(2)}) async-start(), calls=%async_computation.5 | async-start | bytes 1052672 | tf_op jit(solution)/shard_map/all_gather | solution.py:95
  8.6 1484.3 %all-reduce.5.cloned.1.call-start = ((), (), s32[]{:S(2)}) async-start(), calls=%async_computation.6 | async-start | bytes 8388608
  101.2 964.5 %copy-start.2 = (bf16[256,1024]{1,0:T(8,128)(2,1)S(1)}, bf16[256,1024]{1,0:T(8,128)(2,1)}, u32[]{:S(2)}) copy-start(bf16[256,1024]{1,0:T(8,128)(2,1)} %param.15) | copy-start | bytes 1572868
  1081.3 3.9 copy-start
  1099.1 3.9 copy-start
  1116.9 3.9 copy-start
  1134.7 3.9 copy-start
  1152.4 3.9 copy-start
  1170.2 3.9 copy-start
  1188.0 3.9 copy-start
  1205.8 3.9 copy-start
  1216.0 3.3 copy-start.1
  1220.8 361.5 %reduce-scatter.5.cloned.1.call-start = ((), (), s32[]{:S(2)}) async-start(), calls=%async_computation.3 | async-start | bytes 1114112 | tf_op jit(solution)/shard_map/reduce_scatter | solution.py:121
  1223.3 447.0 %reduce-scatter.3.cloned.1.call-start = ((), (), s32[]{:S(2)}) async-start(), calls=%async_computation.2 | async-start | bytes 1114112 | tf_op jit(solution)/shard_map/reduce_scatter | solution.py:120
Sparse Core Ops, SparseCore 0:
  9.8 526.7 all-gather.4
  538.3 525.8 all-gather.6
  1221.0 271.9 all-reduce.4
  1497.3 85.0 reduce-scatter.4
  1586.2 83.9 reduce-scatter.2
where the time goes:
time: 1680 us
  waiting for transfers between devices  1400 us (83%)
  matrix products  104 us (6%)
  blocking collectives  91.2 us (5%)
  local copies, waits for them, and re-layouts  43.5 us (3%)
  other arithmetic  24.2 us (1%)
    all_gather x1, waiting for transfers between devices, on_device(): lax.all_gather(root_values, ('mid', 'leaf'), axis=0, tiled=True)  524 us
    all_gather x1, waiting for transfers between devices, on_device(): lax.all_gather(root_keys, ('mid', 'leaf'), axis=0, tiled=True)  435 us
    unnamed x6, waiting for transfers between devices  265 us
    reduce_scatter x1, waiting for transfers between devices, on_device(): lax.psum_scatter(mid_key_terms, 'leaf', scatter_dimension=0, tiled=True)  87.9 us
    reduce_scatter x1, waiting for transfers between devices, on_device(): lax.psum_scatter(mid_value_terms, 'leaf', scatter_dimension=0, tiled=True)  86.7 us
    all_gather x1, blocking collectives, on_device(): lax.all_gather(mid_keys, 'leaf', axis=0, tiled=True)  49.7 us
    all_gather x1, blocking collectives, on_device(): lax.all_gather(mid_values, 'leaf', axis=0, tiled=True)  41.5 us
    sub x8, matrix products, one_head(): weights = jnp.exp(scores - row_max)  35.3 us
  transfers between devices with their start and end apart: 5, of which 5 were waited for; matrix products, arithmetic and copies ran while one was open for 1% of the time, Pallas kernels for 0%

commit v1 on v0

v1 whole, which is shorter than its diff:
```python
import functools

import jax
import jax.numpy as jnp
from jax import lax
from jax.experimental import pallas as pl
from jax.experimental.pallas import tpu as pltpu
from jax.sharding import PartitionSpec as P

QH = 32
KVH = 8
HD = 128
GROUP = QH // KVH
LEAF = 256
MID = 256
ROOT = 512
KEYS = ROOT + MID + LEAF
HALF = ROOT // 2
OWN = ROOT + MID
CHUNK = 64
AHEAD = 2
FACTOR = HD ** (-0.5)
LOG2E = 1.4426950408889634
MESH = pl.DeviceIdType.MESH
BF = jnp.bfloat16
F32 = jnp.float32


def nt(a, b):
    return lax.dot_general(a, b, (((1,), (1,)), ((), ())), preferred_element_type=F32)


def tn(a, b):
    return lax.dot_general(a, b, (((0,), (0,)), ((), ())), preferred_element_type=F32)


def kernel(
    mid_len, leaf_len, rk, rv, mk, mv, q_hbm, g_hbm, lk_hbm, lv_hbm,
    dq_hbm, dlk_hbm, dlv_hbm, dmk, dmv, drk, drv,
    kv, qb, gb, dqb, dlk, dlv, bias_mid, bias_own, live, s_scr, dp_scr, p_scr, ds_scr,
    shard, gd, gf, rsend, recv_a, bsend, recv_b, msend, recv_x, zsend, recv_z, df, dsend, recv_d,
    load_q, load_g, load_kv, store_sem,
    gd_send, gd_recv, gb_send, gb_recv, ga_send, ga_recv, gz_send, gz_recv, gx_send, gx_recv,
    ra_send, ra_recv, rb_send, rb_recv, rd_send, rd_recv, rx_send, rx_recv, rz_send, rz_recv,
):
    m = lax.axis_index("mid")
    l = lax.axis_index("leaf")
    core = lax.rem(m, 2)
    b = m // 2
    x = l // 4
    z = lax.rem(l, 4)

    def at(mm, ll):
        return {"mid": mm, "leaf": ll}

    sibling = at(m + 1 - 2 * core, l)

    def leaf_peer(d):
        return lax.rem(l + d, 16)

    def b_peer(d):
        return lax.rem(b + d, 8)

    def x_peer(d):
        return lax.rem(x + d, 4)

    def z_peer(d):
        return lax.rem(z + d, 4)

    def send(src, dst, ssem, rsem, device):
        pltpu.make_async_remote_copy(
            src_ref=src, dst_ref=dst, send_sem=ssem, recv_sem=rsem,
            device_id=device, device_id_type=MESH,
        ).start()

    def wait(ref, sem):
        pltpu.make_async_copy(ref, ref, sem).wait()

    def cols(h, width):
        return pl.ds(pl.multiple_of(h * width, width), width)

    for h in range(KVH):
        pltpu.make_async_copy(lk_hbm.at[:, cols(h, HD)], kv.at[h, 0, pl.ds(OWN, LEAF), :], load_kv.at[h]).start()
        pltpu.make_async_copy(lv_hbm.at[:, cols(h, HD)], kv.at[h, 1, pl.ds(OWN, LEAF), :], load_kv.at[h]).start()
        w = GROUP * HD
        pltpu.make_async_copy(q_hbm.at[:, cols(h, w)], qb.at[:, cols(h, w)], load_q.at[h]).start()
        pltpu.make_async_copy(g_hbm.at[:, cols(h, w)], gb.at[:, cols(h, w)], load_g.at[h]).start()

    barrier = pltpu.get_barrier_semaphore()
    for d in range(1, 16):
        pl.semaphore_signal(barrier, inc=1, device_id=at(m, leaf_peer(d)), device_id_type=MESH)
    for d in range(1, 8):
        pl.semaphore_signal(barrier, inc=1, device_id=at(b_peer(d) * 2 + core, l), device_id_type=MESH)
    pl.semaphore_signal(barrier, inc=1, device_id=sibling, device_id_type=MESH)

    for kind, ref in ((0, rk), (1, rv)):
        val = ref[...].astype(F32)
        for r in range(2):
            for h in range(KVH):
                gf[kind, pl.ds(r * KVH + h, 1), :] = val[r : r + 1, h * HD : (h + 1) * HD]
        shard[kind] = gf[kind, pl.ds(0, 16), :].astype(BF)
        gd[l, kind] = shard[kind]
    mid_rows = pl.ds(pl.multiple_of(ROOT + l * 16, 16), 16)
    for kind, ref in ((0, mk), (1, mv)):
        for h in range(KVH):
            kv[h, kind, mid_rows, :] = ref[:, h * HD : (h + 1) * HD]

    pl.semaphore_wait(barrier, 23)

    for d in range(1, 16):
        send(shard, gd.at[l], gd_send, gd_recv, at(m, leaf_peer(d)))
    for h in range(KVH):
        for d in range(1, 4):
            part = kv.at[h, :, mid_rows, :]
            send(part, part, gz_send, gz_recv.at[h], at(m, x * 4 + z_peer(d)))

    mlen = mid_len[0]
    llen = leaf_len[0]
    bias_mid[...] = jnp.where(lax.broadcasted_iota(jnp.int32, (8, MID), 1) < mlen, 0.0, -1e30)
    row = lax.broadcasted_iota(jnp.int32, (LEAF, LEAF), 0)
    col = lax.broadcasted_iota(jnp.int32, (LEAF, LEAF), 1)
    bias_own[...] = jnp.where((col <= row) & (col < llen), 0.0, -1e30)
    live[...] = jnp.where(lax.broadcasted_iota(jnp.int32, (LEAF, HD), 0) < llen, 1.0, 0.0)

    my_rows = pl.ds(pl.multiple_of(core * HALF + b * 32, 32), 32)
    my_half = pl.ds(pl.multiple_of(core * HALF, HALF), HALF)
    other_half = pl.ds(pl.multiple_of((1 - core) * HALF, HALF), HALF)
    x_rows = pl.ds(pl.multiple_of(ROOT + x * 64, 64), 64)

    wait(gd.at[pl.ds(0, 15)], gd_recv)
    for kind in range(2):
        gf[kind] = gd[:, kind].reshape(256, HD).astype(F32)
    for h in range(KVH):
        for kind in range(2):
            kv[h, kind, my_rows, :] = gf[kind, pl.ds(h, 32, stride=KVH), :].astype(BF)
        for d in range(1, 8):
            part = kv.at[h, :, my_rows, :]
            send(part, part, gb_send, gb_recv.at[h], at(b_peer(d) * 2 + core, l))

    def pass_on(h):
        wait(kv.at[h, :, pl.ds(0, 224), :], gb_recv.at[h])
        part = kv.at[h, :, my_half, :]
        send(part, part, ga_send, ga_recv.at[h], sibling)
        wait(kv.at[h, :, pl.ds(ROOT, 48), :], gz_recv.at[h])
        for d in range(1, 4):
            part = kv.at[h, :, x_rows, :]
            send(part, part, gx_send, gx_recv.at[h], at(m, x_peer(d) * 4 + z))

    for h in range(AHEAD):
        pass_on(h)

    def compute(h):
        keys = kv.at[h, 0]
        values = kv.at[h, 1]

        def head_cols(g):
            return pl.ds(pl.multiple_of(h * (GROUP * HD) + g * HD, HD), HD)

        def dots(g):
            s_scr[g] = nt(qb[:, head_cols(g)], keys[...])
            dp_scr[g] = nt(gb[:, head_cols(g)], values[...])

        def soft(g):
            for r0 in range(0, LEAF, CHUNK):
                rows = pl.ds(r0, CHUNK)
                out = pl.ds(g * LEAF + r0, CHUNK)
                s = s_scr[g, rows, :] * (FACTOR * LOG2E)
                s = jnp.concatenate(
                    [s[:, :ROOT], s[:, ROOT:OWN] + bias_mid[0:1, :], s[:, OWN:] + bias_own[rows, :]], 1
                )
                top = jnp.max(s, -1, keepdims=True)
                w = jnp.exp2(s - top)
                p = w * (live[rows, 0:1] / jnp.sum(w, -1, keepdims=True))
                p_scr[out, :] = p.astype(BF)
                dp = dp_scr[g, rows, :]
                dot = jnp.sum(p * dp, -1, keepdims=True)
                ds_scr[out, :] = (p * (dp - dot)).astype(BF)
            dq = jnp.dot(ds_scr[pl.ds(g * LEAF, LEAF), :], keys[...], preferred_element_type=F32)
            dqb[:, head_cols(g)] = (dq * FACTOR).astype(BF)

        dots(0)
        for g in range(GROUP):
            if g + 1 < GROUP:
                dots(g + 1)
            soft(g)
        w = GROUP * HD
        pltpu.make_async_copy(dqb.at[:, cols(h, w)], dq_hbm.at[:, cols(h, w)], store_sem.at[0]).start()
        qs = jnp.concatenate([qb[:, head_cols(g)] for g in range(GROUP)], 0)
        gs = jnp.concatenate([gb[:, head_cols(g)] for g in range(GROUP)], 0)
        dk = tn(qs, ds_scr[...]).T * FACTOR
        dv = tn(gs, p_scr[...]).T
        for kind, val, own in ((0, dk, dlk), (1, dv, dlv)):
            low = val.astype(BF)
            rsend[h, kind] = low[:ROOT]
            msend[h, kind] = low[ROOT:OWN]
            own[:, cols(h, HD)] = low[OWN:]

    def first_sends(h):
        send(rsend.at[h, :, other_half, :], recv_a.at[h], ra_send, ra_recv.at[h], sibling)
        for d in range(1, 4):
            xp = x_peer(d)
            src = msend.at[h, :, pl.ds(pl.multiple_of(xp * 64, 64), 64), :]
            send(src, recv_x.at[h, d - 1], rx_send, rx_recv.at[h], at(m, xp * 4 + z))

    def second_sends(h):
        wait(recv_a.at[h], ra_recv.at[h])
        bsend[h] = (rsend[h, :, my_half, :].astype(F32) + recv_a[h].astype(F32)).astype(BF)
        for d in range(1, 8):
            bp = b_peer(d)
            src = bsend.at[h, :, pl.ds(pl.multiple_of(bp * 32, 32), 32), :]
            send(src, recv_b.at[h, d - 1], rb_send, rb_recv.at[h], at(bp * 2 + core, l))
        wait(recv_x.at[h], rx_recv.at[h])
        own = msend[h, :, pl.ds(pl.multiple_of(x * 64, 64), 64), :].astype(F32)
        zsend[h] = (own + jnp.sum(recv_x[h].astype(F32), 0)).astype(BF)
        for d in range(1, 4):
            zp = z_peer(d)
            src = zsend.at[h, :, pl.ds(pl.multiple_of(zp * 16, 16), 16), :]
            send(src, recv_z.at[h, d - 1], rz_send, rz_recv.at[h], at(m, x * 4 + zp))

    def third_sums(h):
        wait(recv_b.at[h], rb_recv.at[h])
        own = bsend[h, :, pl.ds(pl.multiple_of(b * 32, 32), 32), :].astype(F32)
        total = own + jnp.sum(recv_b[h].astype(F32), 0)
        for kind in range(2):
            df[kind, pl.ds(h, 32, stride=KVH), :] = total[kind]
        wait(recv_z.at[h], rz_recv.at[h])
        own = zsend[h, :, pl.ds(pl.multiple_of(z * 16, 16), 16), :].astype(F32)
        total = own + jnp.sum(recv_z[h].astype(F32), 0)
        dmk[:, cols(h, HD)] = total[0]
        dmv[:, cols(h, HD)] = total[1]

    def step(h, carry):
        @pl.when(h + AHEAD < KVH)
        def _():
            pass_on(h + AHEAD)

        wait(qb.at[:, cols(h, GROUP * HD)], load_q.at[h])
        wait(gb.at[:, cols(h, GROUP * HD)], load_g.at[h])
        wait(kv.at[h, :, pl.ds(OWN, LEAF), :], load_kv.at[h])
        wait(kv.at[h, :, pl.ds(0, HALF), :], ga_recv.at[h])
        wait(kv.at[h, :, pl.ds(0, 192), :], gx_recv.at[h])
        compute(h)
        first_sends(h)

        @pl.when(h >= 1)
        def _():
            second_sends(h - 1)

        @pl.when(h >= 2)
        def _():
            third_sums(h - 2)

        return carry

    lax.fori_loop(0, KVH, step, 0)
    out_k = pltpu.make_async_copy(dlk, dlk_hbm, store_sem.at[1])
    out_v = pltpu.make_async_copy(dlv, dlv_hbm, store_sem.at[2])
    out_k.start()
    out_v.start()
    second_sends(KVH - 1)
    third_sums(KVH - 2)
    third_sums(KVH - 1)

    for kind in range(2):
        dsend[:, kind] = df[kind].astype(BF).reshape(16, 16, HD)
    for d in range(1, 16):
        lp = leaf_peer(d)
        send(dsend.at[lp], recv_d.at[d - 1], rd_send, rd_recv, at(m, lp))
    wait(recv_d, rd_recv)
    total = dsend[l].astype(F32) + jnp.sum(recv_d[...].astype(F32), 0)
    for kind, ref in ((0, drk), (1, drv)):
        for r in range(2):
            for h in range(KVH):
                ref[r : r + 1, h * HD : (h + 1) * HD] = total[kind, r * KVH + h : r * KVH + h + 1]

    wait(dqb, store_sem.at[0])
    out_k.wait()
    out_v.wait()
    wait(gd.at[pl.ds(0, 15)], gd_send)
    wait(kv.at[:, :, pl.ds(0, 224), :], gb_send)
    wait(kv.at[:, :, pl.ds(0, HALF), :], ga_send)
    wait(kv.at[:, :, pl.ds(0, 48), :], gz_send)
    wait(kv.at[:, :, pl.ds(0, 192), :], gx_send)
    wait(recv_a, ra_send)
    wait(recv_b, rb_send)
    wait(recv_d, rd_send)
    wait(recv_x, rx_send)
    wait(recv_z, rz_send)


def on_device(
    queries, out_grad, leaf_keys, leaf_values, mid_keys, mid_values, root_keys, root_values, mid_len, leaf_len
):
    vmem = pl.BlockSpec(memory_space=pltpu.VMEM)
    smem = pl.BlockSpec(memory_space=pltpu.SMEM)
    hbm = pl.BlockSpec(memory_space=pl.ANY)
    kvc = KVH * HD
    dma = pltpu.SemaphoreType.DMA
    one = dma(())
    each = dma((KVH,))
    return pl.pallas_call(
        kernel,
        out_shape=(
            jax.ShapeDtypeStruct((LEAF, QH * HD), BF),
            jax.ShapeDtypeStruct((LEAF, kvc), BF),
            jax.ShapeDtypeStruct((LEAF, kvc), BF),
            jax.ShapeDtypeStruct((16, kvc), F32),
            jax.ShapeDtypeStruct((16, kvc), F32),
            jax.ShapeDtypeStruct((2, kvc), F32),
            jax.ShapeDtypeStruct((2, kvc), F32),
        ),
        in_specs=[smem, smem, vmem, vmem, vmem, vmem, hbm, hbm, hbm, hbm],
        out_specs=(hbm, hbm, hbm, vmem, vmem, vmem, vmem),
        scratch_shapes=[
            pltpu.VMEM((KVH, 2, KEYS, HD), BF),
            pltpu.VMEM((LEAF, QH * HD), BF),
            pltpu.VMEM((LEAF, QH * HD), BF),
            pltpu.VMEM((LEAF, QH * HD), BF),
            pltpu.VMEM((LEAF, kvc), BF),
            pltpu.VMEM((LEAF, kvc), BF),
            pltpu.VMEM((8, MID), F32),
            pltpu.VMEM((LEAF, LEAF), F32),
            pltpu.VMEM((LEAF, HD), F32),
            pltpu.VMEM((GROUP, LEAF, KEYS), F32),
            pltpu.VMEM((GROUP, LEAF, KEYS), F32),
            pltpu.VMEM((GROUP * LEAF, KEYS), BF),
            pltpu.VMEM((GROUP * LEAF, KEYS), BF),
            pltpu.VMEM((2, 16, HD), BF),
            pltpu.VMEM((16, 2, 16, HD), BF),
            pltpu.VMEM((2, 256, HD), F32),
            pltpu.VMEM((KVH, 2, ROOT, HD), BF),
            pltpu.VMEM((KVH, 2, HALF, HD), BF),
            pltpu.VMEM((KVH, 2, HALF, HD), BF),
            pltpu.VMEM((KVH, 7, 2, 32, HD), BF),
            pltpu.VMEM((KVH, 2, MID, HD), BF),
            pltpu.VMEM((KVH, 3, 2, 64, HD), BF),
            pltpu.VMEM((KVH, 2, 64, HD), BF),
            pltpu.VMEM((KVH, 3, 2, 16, HD), BF),
            pltpu.VMEM((2, 256, HD), F32),
            pltpu.VMEM((16, 2, 16, HD), BF),
            pltpu.VMEM((15, 2, 16, HD), BF),
            each, each, each, dma((3,)),
            one, one, one, each, one, each, one, each, one, each,
            one, each, one, each, one, one, one, each, one, each,
        ],
        compiler_params=pltpu.CompilerParams(
            collective_id=0, has_side_effects=True, vmem_limit_bytes=60 * 1024 * 1024
        ),
        cost_estimate=pl.CostEstimate(flops=10 * 2**30, bytes_accessed=8 * 2**20, transcendentals=2**23),
    )(mid_len, leaf_len, root_keys, root_values, mid_keys, mid_values, queries, out_grad, leaf_keys, leaf_values)


def solution(mesh):
    both = P(("mid", "leaf"), None)
    return jax.shard_map(
        on_device,
        mesh=mesh,
        in_specs=(both,) * 8 + (P("mid"), P(("mid", "leaf"))),
        out_specs=(both,) * 7,
        check_vma=False,
    )
```

time: 1680 us -> 90.2 us (0.05)
  waiting for transfers between devices: 1400 us -> 0 us
  matrix products: 104 us -> 0 us
  blocking collectives: 91.2 us -> 0 us
  Pallas kernels: 0 us -> 80.7 us
  local copies, waits for them, and re-layouts: 43.5 us -> 7.28 us
  other arithmetic: 24.2 us -> 0 us
    all_gather x2 -> x0, waiting for transfers between devices: 959 us -> none  [the longest x1 524 us: on_device(): lax.all_gather(root_values, ('mid', 'leaf'), axis=0, tiled=True)]
    unnamed x6 -> x0, waiting for transfers between devices: 265 us -> none
    reduce_scatter x2 -> x0, waiting for transfers between devices: 175 us -> none  [the longest x1 87.9 us: on_device(): lax.psum_scatter(mid_key_terms, 'leaf', scatter_dimension=0, tiled=True)]
    all_gather x2 -> x0, blocking collectives: 91.2 us -> none  [the longest x1 49.7 us: on_device(): lax.all_gather(mid_keys, 'leaf', axis=0, tiled=True)]
    pallas_call x0 -> x1, Pallas kernels: none -> 80.7 us  [on_device(): pl.pallas_call(kernel, out_shape=(jax.ShapeDtypeStruct((LEAF, QH * HD), B...]
    dot_general x32 -> x0, matrix products: 68.6 us -> none  [the longest x8 31.2 us: one_head(): jnp.einsum('gij,igd->jd', probs_low, grad_part, preferred_element_type=jn...]
    sub x8 -> x0, matrix products: 35.3 us -> none  [one_head(): weights = jnp.exp(scores - row_max)]
  transfers between devices with their start and end apart: 5 -> 0, of which waited for: 5 -> 0; matrix products, arithmetic and copies ran while one was open for 1% -> 0% of each run, Pallas kernels for 0% -> 0%
where the time goes in v1:
time: 90.2 us; the launch traced here: 89.9 us
  Pallas kernels  80.7 us (89%)
  local copies, waits for them, and re-layouts  7.28 us (8%)
  between operations  1.97 us (2%)
    pallas_call x1, Pallas kernels, on_device(): pl.pallas_call(kernel, out_shape=(jax.ShapeDtypeStruct((LEAF, QH * HD), B...  80.7 us
    unnamed x19, local copies, waits for them, and re-layouts  7.28 us

profile of v1, /device:TPU:8, one launch (start us, length us, event | category | flops | bytes accessed | tf_op | source)
XLA Modules:
  0.0 89.9 jit_solution(1445616488272931902)
XLA Ops:
  1.9 80.7 %shard_map.153 = (bf16[256,4096]{1,0:T(8,128)(2,1)}, bf16[256,1024]{1,0:T(8,128)(2,1)}, bf16[256,1024]{1,0:T(8,128)(2,1)}, f32[16,1024]{1,0:T(8,128)}, f32[16,10...) custom-call(s32[1]{0:T(128)S(6)} %copy.24.mid_len, s32[1]{0:T(128)S(6)} %copy.25.leaf_len, bf16[2,1024]{1,0:T(2,128)(2,1)} %rk.1, ...), custom_call_target="tpu_custom_call" | custom-call | flops 10737418240 | bytes 8388608 | tf_op jit(solution)/shard_map/pallas_call | solution.py:301
  82.6 0.0 copy-start.1
  82.6 0.0 copy-start
  82.6 3.2 %copy.26 = bf16[256,4096]{1,0:T(8,128)(2,1)} copy(bf16[256,4096]{1,0:T(8,128)(2,1)} %get-tuple-element.14) | data formatting | bytes 4194304
  85.8 0.0 copy-done.1
  85.8 0.0 copy-start.3
  85.8 0.0 copy-start.2
  85.8 0.0 copy-start.5
  85.8 0.0 copy-start.4
  85.9 0.8 copy.27
  86.7 0.0 copy-done
  86.7 0.8 copy.28
  87.4 0.0 copy-done.3
  87.5 0.6 copy.29
  88.1 0.0 copy-done.2
  88.1 0.6 copy.30
  88.7 0.0 copy-done.5
  88.7 0.6 copy.31
  89.3 0.0 copy-done.4
  89.3 0.6 copy.32
Async XLA Ops:
  82.6 3.2 %copy-start.1 = (bf16[256,1024]{1,0:T(8,128)(2,1)S(1)}, bf16[256,1024]{1,0:T(8,128)(2,1)}, u32[]{:S(2)}) copy-start(bf16[256,1024]{1,0:T(8,128)(2,1)} %get-tuple-element.15) | copy-start | bytes 1572868
  82.6 4.0 %copy-start = (bf16[256,1024]{1,0:T(8,128)(2,1)S(1)}, bf16[256,1024]{1,0:T(8,128)(2,1)}, u32[]{:S(2)}) copy-start(bf16[256,1024]{1,0:T(8,128)(2,1)} %get-tuple-element.16) | copy-start | bytes 1572868
  85.8 1.6 %copy-start.3 = (f32[16,1024]{1,0:T(8,128)S(1)}, f32[16,1024]{1,0:T(8,128)}, u32[]{:S(2)}) copy-start(f32[16,1024]{1,0:T(8,128)} %get-tuple-element.17) | copy-start | bytes 196612
  85.8 2.2 %copy-start.2 = (f32[16,1024]{1,0:T(8,128)S(1)}, f32[16,1024]{1,0:T(8,128)}, u32[]{:S(2)}) copy-start(f32[16,1024]{1,0:T(8,128)} %get-tuple-element.18) | copy-start | bytes 196612
  85.8 2.9 %copy-start.5 = (f32[2,1024]{1,0:T(2,128)S(1)}, f32[2,1024]{1,0:T(2,128)}, u32[]{:S(2)}) copy-start(f32[2,1024]{1,0:T(2,128)} %get-tuple-element.19) | copy-start | bytes 24580
  85.8 3.5 %copy-start.4 = (f32[2,1024]{1,0:T(2,128)S(1)}, f32[2,1024]{1,0:T(2,128)}, u32[]{:S(2)}) copy-start(f32[2,1024]{1,0:T(2,128)} %get-tuple-element.20) | copy-start | bytes 24580

commit v2 on v1

v2 whole, which is shorter than its diff:
```python
import functools

import jax
import jax.numpy as jnp
from jax import lax
from jax.experimental import pallas as pl
from jax.experimental.pallas import tpu as pltpu
from jax.sharding import PartitionSpec as P

QH = 32
KVH = 8
HD = 128
GROUP = QH // KVH
LEAF = 256
MID = 256
ROOT = 512
KEYS = ROOT + MID + LEAF
HALF = ROOT // 2
OWN = ROOT + MID
CHUNK = 64
AHEAD = 2
DIRECT = 2
FACTOR = HD ** (-0.5)
LOG2E = 1.4426950408889634
MESH = pl.DeviceIdType.MESH
BF = jnp.bfloat16
F32 = jnp.float32


def nt(a, b):
    return lax.dot_general(a, b, (((1,), (1,)), ((), ())), preferred_element_type=F32)


def tn(a, b):
    return lax.dot_general(a, b, (((0,), (0,)), ((), ())), preferred_element_type=F32)


def kernel(
    mid_len, leaf_len, rk_hbm, rv_hbm, mk_hbm, mv_hbm, q_hbm, g_hbm, lk_hbm, lv_hbm,
    dqb, dlk, dlv, dmk, dmv, drk, drv,
    rk, rv, mk, mv, kv, qb, gb, bias_mid, bias_own, live, s_scr, dp_scr, p_scr, ds_scr,
    shard, gd, gf, rsend, recv_a, bsend, recv_b, recv_y, lsend, recv_l, msend, recv_x, zsend, recv_z, df, dsend, recv_d,
    load_s, load_q, load_g, load_kv,
    gd_send, gd_recv, gb_send, gb_recv, gl_send, gl_recv, gy_send, gy_recv, ga_send, ga_recv, gz_send, gz_recv,
    gx_send, gx_recv, ra_send, ra_recv, rb_send, rb_recv, ry_send, ry_recv, rl_send, rl_recv, rd_send, rd_recv,
    rx_send, rx_recv, rz_send, rz_recv,
):
    m = lax.axis_index("mid")
    l = lax.axis_index("leaf")
    core = lax.rem(m, 2)
    b = m // 2
    x = l // 4
    z = lax.rem(l, 4)
    y = m // 4
    zl = lax.rem(b, 2)

    def at(mm, ll):
        return {"mid": mm, "leaf": ll}

    sibling = at(m + 1 - 2 * core, l)
    next_z = at(m + 2 - 4 * zl, l)

    leaf_ids = {d: lax.rem(l + d, 16) for d in range(1, 16)}
    b_ids = {d: lax.rem(b + d, 8) for d in range(1, 8)}
    x_ids = {d: lax.rem(x + d, 4) for d in range(1, 4)}
    y_ids = {d: lax.rem(y + d, 4) for d in range(1, 4)}
    z_ids = {d: lax.rem(z + d, 4) for d in range(1, 4)}
    leaf_at = {d: at(m, leaf_ids[d]) for d in range(1, 16)}
    b_at = {d: at(b_ids[d] * 2 + core, l) for d in range(1, 8)}
    x_at = {d: at(m, x_ids[d] * 4 + z) for d in range(1, 4)}
    y_at = {d: at(y_ids[d] * 4 + zl * 2 + core, l) for d in range(1, 4)}
    z_at = {d: at(m, x * 4 + z_ids[d]) for d in range(1, 4)}
    b_rows = {d: pl.ds(pl.multiple_of(b_ids[d] * 32, 32), 32) for d in range(1, 8)}
    x_rows_of = {d: pl.ds(pl.multiple_of(x_ids[d] * 64, 64), 64) for d in range(1, 4)}
    y_rows_of = {d: pl.ds(pl.multiple_of(y_ids[d] * 64, 64), 64) for d in range(1, 4)}
    z_rows_of = {d: pl.ds(pl.multiple_of(z_ids[d] * 16, 16), 16) for d in range(1, 4)}
    own_b = pl.ds(pl.multiple_of(b * 32, 32), 32)
    own_x = pl.ds(pl.multiple_of(x * 64, 64), 64)
    own_y = pl.ds(pl.multiple_of(y * 64, 64), 64)
    own_z = pl.ds(pl.multiple_of(z * 16, 16), 16)
    own_l = pl.ds(pl.multiple_of(zl * 32, 32), 32)
    other_l = pl.ds(pl.multiple_of(32 - zl * 32, 32), 32)

    def send(src, dst, ssem, rsem, device):
        pltpu.make_async_remote_copy(
            src_ref=src, dst_ref=dst, send_sem=ssem, recv_sem=rsem,
            device_id=device, device_id_type=MESH,
        ).start()

    def wait(ref, sem):
        pltpu.make_async_copy(ref, ref, sem).wait()

    def cols(h, width):
        return pl.ds(pl.multiple_of(h * width, width), width)

    barrier = pltpu.get_barrier_semaphore()
    for d in range(1, 16):
        pl.semaphore_signal(barrier, inc=1, device_id=leaf_at[d], device_id_type=MESH)
    for d in range(1, 8):
        pl.semaphore_signal(barrier, inc=1, device_id=b_at[d], device_id_type=MESH)
    pl.semaphore_signal(barrier, inc=1, device_id=sibling, device_id_type=MESH)
    small = [
        pltpu.make_async_copy(src, dst, load_s.at[i])
        for i, (src, dst) in enumerate(((rk_hbm, rk), (rv_hbm, rv), (mk_hbm, mk), (mv_hbm, mv)))
    ]
    for copy in small:
        copy.start()
    for copy in small:
        copy.wait()

    for kind, ref in ((0, rk), (1, rv)):
        val = ref[...].astype(F32)
        for r in range(2):
            for h in range(KVH):
                gf[h // 4, pl.ds(kind * 8 + r * 4 + h % 4, 1), :] = val[r : r + 1, h * HD : (h + 1) * HD]
    for half in range(2):
        tile = gf[half, pl.ds(0, 16), :].astype(BF)
        shard[half] = tile
        gd[half, l] = tile
    mid_rows = pl.ds(pl.multiple_of(ROOT + l * 16, 16), 16)
    for kind, ref in ((0, mk), (1, mv)):
        for h in range(KVH):
            kv[h, kind, mid_rows, :] = ref[:, h * HD : (h + 1) * HD]

    pl.semaphore_wait(barrier, 23)

    def send_mid(h0, n, sem):
        part = kv.at[pl.ds(h0, n), :, mid_rows, :]
        for d in range(1, 4):
            send(part, part, gz_send, sem, z_at[d])

    for d in range(1, 16):
        send(shard.at[0], gd.at[0, l], gd_send, gd_recv.at[0], leaf_at[d])
    send_mid(0, DIRECT, gz_recv.at[0])
    for d in range(1, 16):
        send(shard.at[1], gd.at[1, l], gd_send, gd_recv.at[1], leaf_at[d])

    w = GROUP * HD
    for h in range(KVH):
        pltpu.make_async_copy(lk_hbm.at[:, cols(h, HD)], kv.at[h, 0, pl.ds(OWN, LEAF), :], load_kv.at[h]).start()
        pltpu.make_async_copy(lv_hbm.at[:, cols(h, HD)], kv.at[h, 1, pl.ds(OWN, LEAF), :], load_kv.at[h]).start()
        pltpu.make_async_copy(q_hbm.at[:, cols(h, w)], qb.at[:, cols(h, w)], load_q.at[h]).start()
        pltpu.make_async_copy(g_hbm.at[:, cols(h, w)], gb.at[:, cols(h, w)], load_g.at[h]).start()

    mlen = mid_len[0]
    llen = leaf_len[0]
    bias_mid[...] = jnp.where(lax.broadcasted_iota(jnp.int32, (8, MID), 1) < mlen, 0.0, -1e30)
    row = lax.broadcasted_iota(jnp.int32, (LEAF, LEAF), 0)
    col = lax.broadcasted_iota(jnp.int32, (LEAF, LEAF), 1)
    bias_own[...] = jnp.where((col <= row) & (col < llen), 0.0, -1e30)
    live[...] = jnp.where(lax.broadcasted_iota(jnp.int32, (LEAF, HD), 0) < llen, 1.0, 0.0)

    my_rows = pl.ds(pl.multiple_of(core * HALF + b * 32, 32), 32)
    y_rows = pl.ds(pl.multiple_of(core * HALF + y * 64, 64), 64)
    my_half = pl.ds(pl.multiple_of(core * HALF, HALF), HALF)
    other_half = pl.ds(pl.multiple_of((1 - core) * HALF, HALF), HALF)
    x_rows = pl.ds(pl.multiple_of(ROOT + x * 64, 64), 64)

    def unpack(half):
        wait(gd.at[half, pl.ds(0, 15)], gd_recv.at[half])
        gf[half] = gd[half].reshape(256, HD).astype(F32)
        for hh in range(4):
            for kind in range(2):
                kv[half * 4 + hh, kind, my_rows, :] = jnp.concatenate(
                    [gf[half, pl.ds(kind * 8 + r * 4 + hh, 16, stride=16), :] for r in range(2)], 0
                ).astype(BF)

    def share_mid(h0, n):
        part = kv.at[pl.ds(h0, n), :, x_rows, :]
        for d in range(1, 4):
            send(part, part, gx_send, gx_recv.at[h0 // 2], x_at[d])

    def share_half(h):
        part = kv.at[h, :, my_half, :]
        send(part, part, ga_send, ga_recv.at[h], sibling)

    unpack(0)
    for h in range(DIRECT):
        part = kv.at[h, :, my_rows, :]
        for d in range(1, 8):
            send(part, part, gb_send, gb_recv.at[h], b_at[d])
    unpack(1)
    part = kv.at[pl.ds(DIRECT, KVH - DIRECT), :, my_rows, :]
    send(part, part, gl_send, gl_recv, next_z)
    wait(kv.at[pl.ds(0, DIRECT), :, pl.ds(ROOT, 48), :], gz_recv.at[0])
    share_mid(0, 2)
    send_mid(DIRECT, KVH - DIRECT, gz_recv.at[1])
    for h in range(DIRECT):
        wait(kv.at[h, :, pl.ds(0, 224), :], gb_recv.at[h])
        share_half(h)

    def relay():
        wait(kv.at[pl.ds(DIRECT, KVH - DIRECT), :, pl.ds(0, 32), :], gl_recv)
        for h in range(DIRECT, KVH, 2):
            part = kv.at[pl.ds(h, 2), :, y_rows, :]
            for d in range(1, 4):
                send(part, part, gy_send, gy_recv.at[h // 2], y_at[d])
        wait(kv.at[pl.ds(DIRECT, KVH - DIRECT), :, pl.ds(ROOT, 48), :], gz_recv.at[1])
        for h in range(DIRECT, KVH, 2):
            share_mid(h, 2)

    def compute(h):
        keys = kv.at[h, 0]
        values = kv.at[h, 1]

        def head_cols(g):
            return pl.ds(pl.multiple_of(h * (GROUP * HD) + g * HD, HD), HD)

        def dots(g):
            s_scr[g] = nt(qb[:, head_cols(g)], keys[...])
            dp_scr[g] = nt(gb[:, head_cols(g)], values[...])

        def soft(g):
            for r0 in range(0, LEAF, CHUNK):
                rows = pl.ds(r0, CHUNK)
                out = pl.ds(g * LEAF + r0, CHUNK)
                s = s_scr[g, rows, :] * (FACTOR * LOG2E)
                s = jnp.concatenate(
                    [s[:, :ROOT], s[:, ROOT:OWN] + bias_mid[0:1, :], s[:, OWN:] + bias_own[rows, :]], 1
                )
                top = jnp.max(s, -1, keepdims=True)
                w = jnp.exp2(s - top)
                p = w * (live[rows, 0:1] / jnp.sum(w, -1, keepdims=True))
                p_scr[out, :] = p.astype(BF)
                dp = dp_scr[g, rows, :]
                dot = jnp.sum(p * dp, -1, keepdims=True)
                ds_scr[out, :] = (p * (dp - dot)).astype(BF)
            dq = jnp.dot(ds_scr[pl.ds(g * LEAF, LEAF), :], keys[...], preferred_element_type=F32)
            dqb[:, head_cols(g)] = (dq * FACTOR).astype(BF)

        dots(0)
        for g in range(GROUP):
            if g + 1 < GROUP:
                dots(g + 1)
            soft(g)
            if g == 0:
                pl.when(h == 0)(relay)
        qs = jnp.concatenate([qb[:, head_cols(g)] for g in range(GROUP)], 0)
        gs = jnp.concatenate([gb[:, head_cols(g)] for g in range(GROUP)], 0)
        dk = tn(qs, ds_scr[...]).T * FACTOR
        dv = tn(gs, p_scr[...]).T
        for kind, val, own in ((0, dk, dlk), (1, dv, dlv)):
            low = val.astype(BF)
            rsend[h, kind] = low[:ROOT]
            msend[h, kind] = low[ROOT:OWN]
            own[:, cols(h, HD)] = low[OWN:]

    def mid_first(p):
        for d in range(1, 4):
            src = msend.at[pl.ds(2 * p, 2), :, x_rows_of[d], :]
            send(src, recv_x.at[p, d - 1], rx_send, rx_recv.at[p], x_at[d])

    def half_sum(h):
        wait(recv_a.at[h], ra_recv.at[h])
        bsend[h] = (rsend[h, :, my_half, :].astype(F32) + recv_a[h].astype(F32)).astype(BF)

    def mid_second(p):
        wait(recv_x.at[p], rx_recv.at[p])
        pair = pl.ds(2 * p, 2)
        own = msend[pair, :, own_x, :].astype(F32)
        zsend[pair] = (own + jnp.sum(recv_x[p].astype(F32), 0)).astype(BF)
        for d in range(1, 4):
            src = zsend.at[pair, :, z_rows_of[d], :]
            send(src, recv_z.at[p, d - 1], rz_send, rz_recv.at[p], z_at[d])

    def mid_third(p):
        wait(recv_z.at[p], rz_recv.at[p])
        pair = pl.ds(2 * p, 2)
        own = zsend[pair, :, own_z, :].astype(F32)
        total = own + jnp.sum(recv_z[p].astype(F32), 0)
        for i in range(2):
            dmk[:, cols(2 * p + i, HD)] = total[i, 0]
            dmv[:, cols(2 * p + i, HD)] = total[i, 1]

    def keep_root(h, total):
        half = h // 4
        hh = lax.rem(h, 4)
        for kind in range(2):
            for r in range(2):
                df[half, pl.ds(kind * 8 + r * 4 + hh, 16, stride=16), :] = total[kind, r * 16 : (r + 1) * 16]

    def last_sends(half):
        dsend[half] = df[half].astype(BF).reshape(16, 16, HD)
        for d in range(1, 16):
            send(dsend.at[half, leaf_ids[d]], recv_d.at[half, d - 1], rd_send, rd_recv.at[half], leaf_at[d])

    def last_sums(half):
        wait(recv_d.at[half], rd_recv.at[half])
        total = dsend[half, l].astype(F32) + jnp.sum(recv_d[half].astype(F32), 0)
        for kind, ref in ((0, drk), (1, drv)):
            for r in range(2):
                for hh in range(4):
                    row = kind * 8 + r * 4 + hh
                    h = half * 4 + hh
                    ref[r : r + 1, h * HD : (h + 1) * HD] = total[row : row + 1]

    def root_second(h):
        half_sum(h)
        for d in range(1, 4):
            src = bsend.at[h, :, y_rows_of[d], :]
            send(src, recv_y.at[h, d - 1], ry_send, ry_recv.at[h], y_at[d])

    def root_third(h):
        wait(recv_y.at[h], ry_recv.at[h])
        own = bsend[h, :, own_y, :].astype(F32)
        lsend[h] = (own + jnp.sum(recv_y[h].astype(F32), 0)).astype(BF)
        src = lsend.at[h, :, other_l, :]
        send(src, recv_l.at[h], rl_send, rl_recv.at[h], next_z)

    def root_fourth(h):
        wait(recv_l.at[h], rl_recv.at[h])
        own = lsend[h, :, own_l, :].astype(F32)
        keep_root(h, own + recv_l[h].astype(F32))

    def root_second_direct(h):
        half_sum(h)
        at_h = h - (KVH - DIRECT)
        for d in range(1, 8):
            src = bsend.at[h, :, b_rows[d], :]
            send(src, recv_b.at[at_h, d - 1], rb_send, rb_recv.at[at_h], b_at[d])

    def root_third_direct(h):
        at_h = h - (KVH - DIRECT)
        wait(recv_b.at[at_h], rb_recv.at[at_h])
        own = bsend[h, :, own_b, :].astype(F32)
        keep_root(h, own + jnp.sum(recv_b[at_h].astype(F32), 0))

    def step(h, carry):
        wait(qb.at[:, cols(h, GROUP * HD)], load_q.at[h])
        wait(gb.at[:, cols(h, GROUP * HD)], load_g.at[h])
        wait(kv.at[h, :, pl.ds(OWN, LEAF), :], load_kv.at[h])
        wait(kv.at[h, :, pl.ds(0, HALF), :], ga_recv.at[h])

        @pl.when(lax.rem(h, 2) == 0)
        def _():
            wait(kv.at[pl.ds(0, 2), :, pl.ds(0, 192), :], gx_recv.at[h // 2])

        compute(h)
        send(rsend.at[h, :, other_half, :], recv_a.at[h], ra_send, ra_recv.at[h], sibling)

        @pl.when(h + AHEAD < KVH)
        def _():
            @pl.when(lax.rem(h, 2) == 0)
            def _():
                wait(kv.at[pl.ds(0, 2), :, pl.ds(0, 192), :], gy_recv.at[h // 2 + 1])

            share_half(h + AHEAD)

        @pl.when(lax.rem(h, 2) == 1)
        def _():
            mid_first(h // 2)

        @pl.when((h >= 1) & (h < KVH - 1))
        def _():
            root_second(h - 1)

        @pl.when((h >= 2) & (lax.rem(h, 2) == 0))
        def _():
            mid_second(h // 2 - 1)

        @pl.when(h >= 2)
        def _():
            root_third(h - 2)

        @pl.when((h >= 3) & (lax.rem(h, 2) == 1))
        def _():
            mid_third(h // 2 - 1)

        @pl.when(h >= 3)
        def _():
            root_fourth(h - 3)

        @pl.when(h == 6)
        def _():
            last_sends(0)

        return carry

    lax.fori_loop(0, KVH, step, 0)
    root_second_direct(KVH - 2)
    root_second_direct(KVH - 1)
    mid_second(3)
    root_fourth(KVH - 3)
    root_third_direct(KVH - 2)
    last_sums(0)
    root_third_direct(KVH - 1)
    last_sends(1)
    mid_third(3)
    last_sums(1)

    wait(gd.at[:, pl.ds(0, 15)], gd_send)
    wait(kv.at[pl.ds(0, DIRECT), :, pl.ds(0, 224), :], gb_send)
    wait(kv.at[pl.ds(0, KVH - DIRECT), :, pl.ds(0, 32), :], gl_send)
    wait(kv.at[pl.ds(0, KVH - DIRECT), :, pl.ds(0, 192), :], gy_send)
    wait(kv.at[:, :, pl.ds(0, HALF), :], ga_send)
    wait(kv.at[:, :, pl.ds(0, 48), :], gz_send)
    wait(kv.at[:, :, pl.ds(0, 192), :], gx_send)
    wait(recv_a, ra_send)
    wait(recv_b, rb_send)
    wait(recv_y, ry_send)
    wait(recv_l, rl_send)
    wait(recv_d, rd_send)
    wait(recv_x, rx_send)
    wait(recv_z, rz_send)


OUTS = (
    ((LEAF, QH * HD), BF),
    ((LEAF, KVH * HD), BF),
    ((LEAF, KVH * HD), BF),
    ((16, KVH * HD), F32),
    ((16, KVH * HD), F32),
    ((2, KVH * HD), F32),
    ((2, KVH * HD), F32),
)


def place(*refs):
    sems = refs[-1]
    copies = [pltpu.make_async_copy(refs[i], refs[7 + i], sems.at[i]) for i in range(7)]
    for c in copies:
        c.start()
    for c in copies:
        c.wait()


def on_device(
    queries, out_grad, leaf_keys, leaf_values, mid_keys, mid_values, root_keys, root_values, mid_len, leaf_len
):
    vmem = pl.BlockSpec(memory_space=pltpu.VMEM)
    smem = pl.BlockSpec(memory_space=pltpu.SMEM)
    hbm = pl.BlockSpec(memory_space=pl.ANY)
    kvc = KVH * HD
    dma = pltpu.SemaphoreType.DMA
    one = dma(())
    two = dma((2,))
    each = dma((KVH,))
    outs = pl.pallas_call(
        kernel,
        out_shape=tuple(pltpu.VMEM(*o) for o in OUTS),
        in_specs=[smem, smem] + [hbm] * 8,
        out_specs=(vmem,) * 7,
        scratch_shapes=[
            pltpu.VMEM((2, kvc), BF),
            pltpu.VMEM((2, kvc), BF),
            pltpu.VMEM((16, kvc), BF),
            pltpu.VMEM((16, kvc), BF),
            pltpu.VMEM((KVH, 2, KEYS, HD), BF),
            pltpu.VMEM((LEAF, QH * HD), BF),
            pltpu.VMEM((LEAF, QH * HD), BF),
            pltpu.VMEM((8, MID), F32),
            pltpu.VMEM((LEAF, LEAF), F32),
            pltpu.VMEM((LEAF, HD), F32),
            pltpu.VMEM((GROUP, LEAF, KEYS), F32),
            pltpu.VMEM((GROUP, LEAF, KEYS), F32),
            pltpu.VMEM((GROUP * LEAF, KEYS), BF),
            pltpu.VMEM((GROUP * LEAF, KEYS), BF),
            pltpu.VMEM((2, 16, HD), BF),
            pltpu.VMEM((2, 16, 16, HD), BF),
            pltpu.VMEM((2, 256, HD), F32),
            pltpu.VMEM((KVH, 2, ROOT, HD), BF),
            pltpu.VMEM((KVH, 2, HALF, HD), BF),
            pltpu.VMEM((KVH, 2, HALF, HD), BF),
            pltpu.VMEM((DIRECT, 7, 2, 32, HD), BF),
            pltpu.VMEM((KVH - DIRECT, 3, 2, 64, HD), BF),
            pltpu.VMEM((KVH - DIRECT, 2, 64, HD), BF),
            pltpu.VMEM((KVH - DIRECT, 2, 32, HD), BF),
            pltpu.VMEM((KVH, 2, MID, HD), BF),
            pltpu.VMEM((KVH // 2, 3, 2, 2, 64, HD), BF),
            pltpu.VMEM((KVH, 2, 64, HD), BF),
            pltpu.VMEM((KVH // 2, 3, 2, 2, 16, HD), BF),
            pltpu.VMEM((2, 256, HD), F32),
            pltpu.VMEM((2, 16, 16, HD), BF),
            pltpu.VMEM((2, 15, 16, HD), BF),
            dma((4,)), each, each, each,
            one, two, one, each, one, one, one, each, one, each, one, two,
            one, each, one, each, one, each, one, each, one, each, one, two,
            one, each, one, each,
        ],
        compiler_params=pltpu.CompilerParams(
            collective_id=0, has_side_effects=True, vmem_limit_bytes=60 * 1024 * 1024
        ),
        cost_estimate=pl.CostEstimate(flops=10 * 2**30, bytes_accessed=8 * 2**20, transcendentals=2**23),
    )(mid_len, leaf_len, root_keys, root_values, mid_keys, mid_values, queries, out_grad, leaf_keys, leaf_values)
    return pl.pallas_call(
        place,
        out_shape=tuple(jax.ShapeDtypeStruct(*o) for o in OUTS),
        in_specs=[vmem] * 7,
        out_specs=(hbm,) * 7,
        scratch_shapes=[dma((7,))],
        compiler_params=pltpu.CompilerParams(vmem_limit_bytes=4 * 1024 * 1024),
    )(*outs)


def solution(mesh):
    both = P(("mid", "leaf"), None)
    return jax.shard_map(
        on_device,
        mesh=mesh,
        in_specs=(both,) * 8 + (P("mid"), P(("mid", "leaf"))),
        out_specs=(both,) * 7,
        check_vma=False,
    )
```

time: 90.2 us -> 81.2 us (0.900); the launches traced: 89.9 us -> 79.8 us
  local copies, waits for them, and re-layouts: 7.28 us -> 0 us
  Pallas kernels: 80.7 us -> 77.9 us
    unnamed x19 -> x0, local copies, waits for them, and re-layouts: 7.28 us -> none
    pallas_call x1 -> x2, Pallas kernels: 80.7 us -> 77.9 us  [the longest x1 76.2 us: on_device(): pl.pallas_call(kernel, out_shape=tuple((pltpu.VMEM(*o) for o in OUTS)), i...]
where the time goes in v2:
time: 81.2 us; the launch traced here: 79.8 us
  Pallas kernels  77.9 us (96%)
  between operations  1.94 us (2%)
    pallas_call x1, Pallas kernels, on_device(): pl.pallas_call(kernel, out_shape=tuple((pltpu.VMEM(*o) for o in OUTS)), i...  76.2 us
    pallas_call x1, Pallas kernels, on_device(): pl.pallas_call(place, out_shape=tuple((jax.ShapeDtypeStruct(*o) for o in...  1.75 us

profile of v2, /device:TPU:8, one launch (start us, length us, event | category | flops | bytes accessed | tf_op | source)
XLA Modules:
  0.0 79.8 jit_solution(12882131177455027973)
XLA Ops:
  1.9 76.2 %shard_map.153 = (bf16[256,4096]{1,0:T(8,128)(2,1)S(1)}, bf16[256,1024]{1,0:T(8,128)(2,1)S(1)}, bf16[256,1024]{1,0:T(8,128)(2,1)S(1)}, f32[16,1024]{1,0:T(8,128)...) custom-call(s32[1]{0:T(128)S(6)} %copy.17.mid_len, s32[1]{0:T(128)S(6)} %copy.18.leaf_len, ...), custom_call_target="tpu_custom_call" | custom-call | flops 10737418240 | bytes 8388608 | tf_op jit(solution)/shard_map/pallas_call | solution.py:438
  78.1 1.8 %shard_map.154 = (bf16[256,4096]{1,0:T(8,128)(2,1)}, bf16[256,1024]{1,0:T(8,128)(2,1)}, bf16[256,1024]{1,0:T(8,128)(2,1)}, f32[16,1024]{1,0:T(8,128)}, f32[16,10...) custom-call(bf16[256,4096]{1,0:T(8,128)(2,1)S(1)} %get-tuple-element.14.refs_0_, ...), custom_call_target="tpu_custom_call" | custom-call | tf_op jit(solution)/shard_map/pallas_call | solution.py:485

commit v3 on v2

--- a/solution.py
+++ b/solution.py
@@ -38,7 +38,7 @@
 def kernel(
     mid_len, leaf_len, rk_hbm, rv_hbm, mk_hbm, mv_hbm, q_hbm, g_hbm, lk_hbm, lv_hbm,
     dqb, dlk, dlv, dmk, dmv, drk, drv,
-    rk, rv, mk, mv, kv, qb, gb, bias_mid, bias_own, live, s_scr, dp_scr, p_scr, ds_scr,
+    rk, rv, mk, mv, kv, qb, gb, bias_mid, bias_own, live, s_scr, dp_scr, p_scr, ds_all,
     shard, gd, gf, rsend, recv_a, bsend, recv_b, recv_y, lsend, recv_l, msend, recv_x, zsend, recv_z, df, dsend, recv_d,
     load_s, load_q, load_g, load_kv,
     gd_send, gd_recv, gb_send, gb_recv, gl_send, gl_recv, gy_send, gy_recv, ga_send, ga_recv, gz_send, gz_recv,
@@ -142,6 +142,11 @@
         pltpu.make_async_copy(q_hbm.at[:, cols(h, w)], qb.at[:, cols(h, w)], load_q.at[h]).start()
         pltpu.make_async_copy(g_hbm.at[:, cols(h, w)], gb.at[:, cols(h, w)], load_g.at[h]).start()
 
+    for g in range(GROUP):
+        p_scr[pl.ds(g * LEAF, HD), pl.ds(KEYS - HD, HD)] = jnp.zeros((HD, HD), BF)
+        for h in range(KVH):
+            ds_all[h, pl.ds(g * LEAF, HD), pl.ds(KEYS - HD, HD)] = jnp.zeros((HD, HD), BF)
+
     mlen = mid_len[0]
     llen = leaf_len[0]
     bias_mid[...] = jnp.where(lax.broadcasted_iota(jnp.int32, (8, MID), 1) < mlen, 0.0, -1e30)
@@ -158,7 +163,7 @@
 
     def unpack(half):
         wait(gd.at[half, pl.ds(0, 15)], gd_recv.at[half])
-        gf[half] = gd[half].reshape(256, HD).astype(F32)
+        gf[half, pl.ds(0, 256), :] = gd[half].reshape(256, HD).astype(F32)
         for hh in range(4):
             for kind in range(2):
                 kv[half * 4 + hh, kind, my_rows, :] = jnp.concatenate(
@@ -200,6 +205,7 @@
             share_mid(h, 2)
 
     def compute(h):
+        ds_scr = ds_all.at[h]
         keys = kv.at[h, 0]
         values = kv.at[h, 1]
 
@@ -214,19 +220,19 @@
             for r0 in range(0, LEAF, CHUNK):
                 rows = pl.ds(r0, CHUNK)
                 out = pl.ds(g * LEAF + r0, CHUNK)
-                s = s_scr[g, rows, :] * (FACTOR * LOG2E)
+                width = KEYS if r0 + CHUNK > HD else KEYS - HD
+                used = pl.ds(0, width)
+                s = s_scr[g, rows, used] * (FACTOR * LOG2E)
                 s = jnp.concatenate(
-                    [s[:, :ROOT], s[:, ROOT:OWN] + bias_mid[0:1, :], s[:, OWN:] + bias_own[rows, :]], 1
+                    [s[:, :ROOT], s[:, ROOT:OWN] + bias_mid[0:1, :], s[:, OWN:] + bias_own[rows, 0 : width - OWN]], 1
                 )
                 top = jnp.max(s, -1, keepdims=True)
                 w = jnp.exp2(s - top)
                 p = w * (live[rows, 0:1] / jnp.sum(w, -1, keepdims=True))
-                p_scr[out, :] = p.astype(BF)
-                dp = dp_scr[g, rows, :]
+                p_scr[out, used] = p.astype(BF)
+                dp = dp_scr[g, rows, used]
                 dot = jnp.sum(p * dp, -1, keepdims=True)
-                ds_scr[out, :] = (p * (dp - dot)).astype(BF)
-            dq = jnp.dot(ds_scr[pl.ds(g * LEAF, LEAF), :], keys[...], preferred_element_type=F32)
-            dqb[:, head_cols(g)] = (dq * FACTOR).astype(BF)
+                ds_scr[out, used] = (p * (dp - dot)).astype(BF)
 
         dots(0)
         for g in range(GROUP):
@@ -245,6 +251,16 @@
             msend[h, kind] = low[ROOT:OWN]
             own[:, cols(h, HD)] = low[OWN:]
 
+    def query_grads(first, last):
+        def one(h, carry):
+            for g in range(GROUP):
+                dq = jnp.dot(ds_all[h, pl.ds(g * LEAF, LEAF), :], kv[h, 0], preferred_element_type=F32)
+                out = pl.ds(pl.multiple_of(h * (GROUP * HD) + g * HD, HD), HD)
+                dqb[:, out] = (dq * FACTOR).astype(BF)
+            return carry
+
+        lax.fori_loop(first, last, one, 0)
+
     def mid_first(p):
         for d in range(1, 4):
             src = msend.at[pl.ds(2 * p, 2), :, x_rows_of[d], :]
@@ -280,7 +296,7 @@
                 df[half, pl.ds(kind * 8 + r * 4 + hh, 16, stride=16), :] = total[kind, r * 16 : (r + 1) * 16]
 
     def last_sends(half):
-        dsend[half] = df[half].astype(BF).reshape(16, 16, HD)
+        dsend[half] = df[half, pl.ds(0, 256), :].astype(BF).reshape(16, 16, HD)
         for d in range(1, 16):
             send(dsend.at[half, leaf_ids[d]], recv_d.at[half, d - 1], rd_send, rd_recv.at[half], leaf_at[d])
 
@@ -378,13 +394,16 @@
 
     lax.fori_loop(0, KVH, step, 0)
     root_second_direct(KVH - 2)
+    query_grads(0, 1)
     root_second_direct(KVH - 1)
     mid_second(3)
     root_fourth(KVH - 3)
+    query_grads(1, 5)
     root_third_direct(KVH - 2)
     last_sums(0)
     root_third_direct(KVH - 1)
     last_sends(1)
+    query_grads(5, KVH)
     mid_third(3)
     last_sums(1)
 
@@ -454,10 +473,10 @@
             pltpu.VMEM((GROUP, LEAF, KEYS), F32),
             pltpu.VMEM((GROUP, LEAF, KEYS), F32),
             pltpu.VMEM((GROUP * LEAF, KEYS), BF),
-            pltpu.VMEM((GROUP * LEAF, KEYS), BF),
+            pltpu.VMEM((KVH, GROUP * LEAF, KEYS), BF),
             pltpu.VMEM((2, 16, HD), BF),
             pltpu.VMEM((2, 16, 16, HD), BF),
-            pltpu.VMEM((2, 256, HD), F32),
+            pltpu.VMEM((2, 272, HD), F32),
             pltpu.VMEM((KVH, 2, ROOT, HD), BF),
             pltpu.VMEM((KVH, 2, HALF, HD), BF),
             pltpu.VMEM((KVH, 2, HALF, HD), BF),
@@ -469,7 +488,7 @@
             pltpu.VMEM((KVH // 2, 3, 2, 2, 64, HD), BF),
             pltpu.VMEM((KVH, 2, 64, HD), BF),
             pltpu.VMEM((KVH // 2, 3, 2, 2, 16, HD), BF),
-            pltpu.VMEM((2, 256, HD), F32),
+            pltpu.VMEM((2, 272, HD), F32),
             pltpu.VMEM((2, 16, 16, HD), BF),
             pltpu.VMEM((2, 15, 16, HD), BF),
             dma((4,)), each, each, each,

time: 81.2 us -> 79.2 us (0.975); the launches traced: 79.8 us -> 79 us
  no operation moved by 1% of the time
where the time goes in v3:
time: 79.2 us; the launch traced here: 79 us
  Pallas kernels  77.1 us (97%)
  between operations  1.94 us (2%)
    pallas_call x1, Pallas kernels, on_device(): pl.pallas_call(kernel, out_shape=tuple((pltpu.VMEM(*o) for o in OUTS)), i...  75.4 us
    pallas_call x1, Pallas kernels, on_device(): pl.pallas_call(place, out_shape=tuple((jax.ShapeDtypeStruct(*o) for o in...  1.75 us

profile of v3, /device:TPU:8, one launch (start us, length us, event | category | flops | bytes accessed | tf_op | source)
XLA Modules:
  0.0 79.0 jit_solution(8957932599743171819)
XLA Ops:
  1.9 75.4 %shard_map.153 = (bf16[256,4096]{1,0:T(8,128)(2,1)S(1)}, bf16[256,1024]{1,0:T(8,128)(2,1)S(1)}, bf16[256,1024]{1,0:T(8,128)(2,1)S(1)}, f32[16,1024]{1,0:T(8,128)...) custom-call(s32[1]{0:T(128)S(6)} %copy.17.mid_len, s32[1]{0:T(128)S(6)} %copy.18.leaf_len, ...), custom_call_target="tpu_custom_call" | custom-call | flops 10737418240 | bytes 8388608 | tf_op jit(solution)/shard_map/pallas_call | solution.py:457
  77.3 1.8 %shard_map.154 = (bf16[256,4096]{1,0:T(8,128)(2,1)}, bf16[256,1024]{1,0:T(8,128)(2,1)}, bf16[256,1024]{1,0:T(8,128)(2,1)}, f32[16,1024]{1,0:T(8,128)}, f32[16,10...) custom-call(bf16[256,4096]{1,0:T(8,128)(2,1)S(1)} %get-tuple-element.14.refs_0_, ...), custom_call_target="tpu_custom_call" | custom-call | tf_op jit(solution)/shard_map/pallas_call | solution.py:504
